TPU v7x, 32 devices: a whole 2x2x4 slice. The times are simulated.
32 devices in a mesh: node: 8 (over y, x, core), local: 4 (over z).
Axes of the slice: x: 2, y: 2, z: 4, core: 2. Of those that a mesh axis runs over, the one named last changes fastest.
Arguments:
- tokens: bfloat16 [1024, 7168], P('node', 'local'), may hold values from -6 to 6
- out_grad: bfloat16 [1024, 7168], P('node', 'local'), may hold values from -6 to 6
- expert_ids: int32 [1024, 8], P('node'), may hold values from 0 to 15, as said below
- gates: float32 [1024, 8], P('node'), may hold values from 0.05 to 1
- gate_weight: bfloat16 [16, 7168, 1024], P('node', 'local'), may hold values from -0.0625 to 0.0625
- up_weight: bfloat16 [16, 7168, 1024], P('node', 'local'), may hold values from -0.0625 to 0.0625
- down_weight: bfloat16 [16, 1024, 7168], P('node', None, 'local'), may hold values from -0.1875 to 0.1875
Outputs:
- grad_tokens: bfloat16 [1024, 7168], P('node', 'local')
- gate_grad: bfloat16 [16, 7168, 1024], P('node', 'local')
- up_grad: bfloat16 [16, 7168, 1024], P('node', 'local')
- down_grad: bfloat16 [16, 1024, 7168], P('node', None, 'local')
Inputs may be any that keep to these rules, and one draw needn't show every extreme that they name: `expert_ids`: each row names 8 different experts, all within at most 4 routing groups, group g being experts g * 4 to g * 4 + 3.
All inputs are finite; a program needn't handle non-finite values.
Results may differ from a plain program's by a relative error of at most 0.029.
Values may be sent and summed in bfloat16 or wider, within the bound.
A program may use at most 128 MiB of HBM per device.

v0:
```python
import jax
import jax.numpy as jnp
from jax import lax
from jax.sharding import PartitionSpec as P


def swiglu_backward(gate_pre, up_pre, grad_hidden):
    sigmoid_g = jax.nn.sigmoid(gate_pre)
    activated = gate_pre * sigmoid_g
    hidden_act = (activated * up_pre).astype(jnp.bfloat16)
    grad_gate = (grad_hidden * up_pre * sigmoid_g * (1.0 + gate_pre * (1.0 - sigmoid_g))).astype(
        jnp.bfloat16
    )
    grad_up = (grad_hidden * activated).astype(jnp.bfloat16)
    return (hidden_act, grad_gate, grad_up)


def on_device(tokens, out_grad, expert_ids, gates, gate_weight, up_weight, down_weight):
    tok_rows, slice_width = tokens.shape
    top_count = expert_ids.shape[1]
    node_count = lax.axis_size("node")
    exp_local = gate_weight.shape[0]
    hidden = gate_weight.shape[2]
    experts = exp_local * node_count
    capacity = tok_rows * top_count * 5 // (experts * 4)
    row_count = node_count * capacity
    flat_ids = expert_ids.reshape(-1)
    onehot = (flat_ids[:, None] == jnp.arange(experts, dtype=jnp.int32)[None, :]).astype(jnp.int32)
    earlier = jnp.cumsum(onehot, axis=0) - onehot
    slot_pos = jnp.sum(earlier * onehot, axis=1)
    kept_mask = slot_pos < capacity
    owner_node = flat_ids // exp_local
    within = flat_ids % exp_local
    dest_row = jnp.where(
        kept_mask, (within * node_count + owner_node) * capacity + slot_pos, experts * capacity
    )
    x_rep = jnp.repeat(tokens, top_count, axis=0)
    dy_rep = (
        gates.reshape(-1, 1) * jnp.repeat(out_grad, top_count, axis=0).astype(jnp.float32)
    ).astype(jnp.bfloat16)
    blank = jnp.zeros((experts * capacity, slice_width), jnp.bfloat16)
    x_send = (
        blank.at[dest_row]
        .set(x_rep, mode="drop")
        .reshape(exp_local, node_count, capacity, slice_width)
    )
    dy_send = (
        blank.at[dest_row]
        .set(dy_rep, mode="drop")
        .reshape(exp_local, node_count, capacity, slice_width)
    )
    x_recv, dy_recv = (
        lax.all_to_all(x_send, "node", split_axis=1, concat_axis=1, tiled=True),
        lax.all_to_all(dy_send, "node", split_axis=1, concat_axis=1, tiled=True),
    )
    gate_pre = jnp.einsum("enrd,edf->enrf", x_recv, gate_weight, preferred_element_type=jnp.float32)
    up_pre = jnp.einsum("enrd,edf->enrf", x_recv, up_weight, preferred_element_type=jnp.float32)
    grad_hidden = jnp.einsum(
        "enrd,efd->enrf", dy_recv, down_weight, preferred_element_type=jnp.float32
    )
    stacked = jnp.stack((gate_pre, up_pre, grad_hidden), axis=3)
    x_flat = x_recv.reshape(exp_local, row_count, slice_width)
    dy_flat = dy_recv.reshape(exp_local, row_count, slice_width)
    stacked = stacked.reshape(exp_local, row_count, 3, hidden)
    totals = lax.psum(stacked.astype(jnp.bfloat16), "local").astype(jnp.float32)
    hidden_act, grad_gate, grad_up = swiglu_backward(
        totals[:, :, 0], totals[:, :, 1], totals[:, :, 2]
    )
    down_grad = jnp.einsum(
        "erf,erd->efd", hidden_act, dy_flat, preferred_element_type=jnp.float32
    ).astype(jnp.bfloat16)
    gate_grad = jnp.einsum(
        "erd,erf->edf", x_flat, grad_gate, preferred_element_type=jnp.float32
    ).astype(jnp.bfloat16)
    up_grad = jnp.einsum(
        "erd,erf->edf", x_flat, grad_up, preferred_element_type=jnp.float32
    ).astype(jnp.bfloat16)
    grad_rows = (
        jnp.einsum("erf,edf->erd", grad_gate, gate_weight, preferred_element_type=jnp.float32)
        + jnp.einsum("erf,edf->erd", grad_up, up_weight, preferred_element_type=jnp.float32)
    ).astype(jnp.bfloat16)
    returned = lax.all_to_all(
        grad_rows.reshape(exp_local, node_count, capacity, slice_width),
        "node",
        split_axis=1,
        concat_axis=1,
        tiled=True,
    )
    back_rows = returned.reshape(experts * capacity, slice_width)
    safe_row = jnp.minimum(dest_row, experts * capacity - 1)
    picked = jnp.where(
        kept_mask[:, None], back_rows[safe_row].astype(jnp.float32), jnp.float32(0.0)
    )
    grad_tokens = picked.reshape(tok_rows, top_count, slice_width).sum(axis=1).astype(jnp.bfloat16)
    return (grad_tokens, gate_grad, up_grad, down_grad)


def solution(mesh):
    return jax.shard_map(
        on_device,
        mesh=mesh,
        in_specs=(
            P("node", "local"),
            P("node", "local"),
            P("node", None),
            P("node", None),
            P("node", "local", None),
            P("node", "local", None),
            P("node", None, "local"),
        ),
        out_specs=(
            P("node", "local"),
            P("node", "local", None),
            P("node", "local", None),
            P("node", None, "local"),
        ),
        check_vma=False,
    )
```

profile of v0, /device:TPU:0, one launch (start us, length us, event | category | flops | bytes accessed | tf_op | source)
XLA Modules:
  0.0 592.6 jit_solution(8184263110759701689)
XLA Ops:
  8.3 4.5 reduce-window.6
  15.3 9.1 %scatter_custom_fusion.1 = bf16[1280,1792]{1,0:T(8,128)(2,1)} fusion(s32[1024]{0:T(1024)S(1)} %bitcast.111, f32[128,1792]{1,0:T(8,128)S(1)} %convert_element_type.54, f32[1024]{0:T(1024)S(1)} %mul.69, bf16[]{:T(256)} %constant.38.clone.1), kind=kCustom, calls=%fused_computation.26 | custom fusion | flops 3670016 | bytes 5509122 | tf_op jit(solution)/shard_map/scatter | solution.py:49
  24.5 4.8 copy.66
  29.2 5.2 all-to-all-start.1
  34.4 8.7 %scatter_custom_fusion = bf16[1280,1792]{1,0:T(8,128)(2,1)} fusion(s32[1024]{0:T(1024)S(1)} %bitcast.112, bf16[]{:T(256)} %constant.38.clone.1, bf16[128,1792]{1,0:T(8,128)(2,1)S(1)} %copy-done), kind=kCustom, calls=%fused_computation.27 | custom fusion | bytes 5046274 | tf_op jit(solution)/shard_map/scatter | solution.py:44
  43.2 4.8 copy.62
  47.9 39.9 %all-to-all-done.1 = bf16[2,8,80,1792]{3,2,0,1:T(8,128)(2,1)} async-done(((bf16[2,8,80,1792]{3,2,0,1:T(8,128)(2,1)}), bf16[2,8,80,1792]{3,2,0,1:T(8,128)(2,1)}, u32[]{:S(2)}, u32[]{:S(2)}) %all-to-all-start.1) | async-done | bytes 4587552 | tf_op jit(solution)/shard_map/all_to_all | solution.py:54
  87.8 5.1 all-to-all-start
  93.0 10.9 %fusion.23 = bf16[2,8,80,1024]{3,2,1,0:T(8,128)(2,1)} fusion(bf16[2,1024,1792]{2,1,0:T(8,128)(2,1)} %param.13, bf16[2,8,80,1792]{3,2,0,1:T(8,128)(2,1)} %all-to-all-done.1), kind=kOutput, calls=%fused_computation.35 | convolution fusion | flops 4698931200 | bytes 14548992 | tf_op jit(solution)/shard_map/enrd,efd->enrf/dot_general | solution.py:58
  103.9 3.1 copy.70
  107.0 39.2 %all-to-all-done = bf16[2,8,80,1792]{3,2,0,1:T(8,128)(2,1)} async-done(((bf16[2,8,80,1792]{3,2,0,1:T(8,128)(2,1)}), bf16[2,8,80,1792]{3,2,0,1:T(8,128)(2,1)}, u32[]{:S(2)}, u32[]{:S(2)}) %all-to-all-start) | async-done | bytes 4587552 | tf_op jit(solution)/shard_map/all_to_all | solution.py:53
  146.3 10.9 %fusion.17 = bf16[2,8,80,1024]{3,2,1,0:T(8,128)(2,1)} fusion(bf16[2,1792,1024]{2,1,0:T(8,128)(2,1)} %param.11, bf16[2,8,80,1792]{3,2,0,1:T(8,128)(2,1)} %all-to-all-done), kind=kOutput, calls=%fused_computation.33 | convolution fusion | flops 4698931200 | bytes 14548992 | tf_op jit(solution)/shard_map/enrd,edf->enrf/dot_general | solution.py:56
  157.2 4.4 copy.68
  161.5 10.9 %fusion.20 = bf16[2,8,80,1024]{3,2,1,0:T(8,128)(2,1)} fusion(bf16[2,1792,1024]{2,1,0:T(8,128)(2,1)} %param.12, bf16[2,8,80,1792]{3,2,0,1:T(8,128)(2,1)} %all-to-all-done), kind=kOutput, calls=%fused_computation.34 | convolution fusion | flops 4698931200 | bytes 14548992 | tf_op jit(solution)/shard_map/enrd,edf->enrf/dot_general | solution.py:57
  172.4 4.4 copy.69
  176.8 6.3 %pad_maximum_fusion = bf16[2,640,3,1024]{1,3,0,2:T(8,128)(2,1)} fusion(bf16[2,640,1,1024]{1,3,0,2:T(8,128)(2,1)S(1)} %copy.70, bf16[2,640,1,1024]{1,3,0,2:T(8,128)(2,1)} %copy.69, bf16[2,640,1,1024]{1,3,0,2:T(8,128)(2,1)} %copy.68), kind=kLoop, calls=%fused_computation.4 | loop fusion | flops 7864320 | bytes 15728640 | tf_op jit(solution)/shard_map/stack | solution.py:61
  183.1 274.1 %all-reduce.2.cloned.1.call-done = bf16[2,640,3,1024]{1,3,0,2:T(8,128)(2,1)} async-done(((bf16[2,640,3,1024]{1,3,0,2:T(8,128)(2,1)}), bf16[2,640,3,1024]{1,3,0,2:T(8,128)(2,1)}) %all-reduce.2.cloned.1.call-update) | async-done | bytes 7864336 | tf_op jit(solution)/shard_map/psum | solution.py:65
  457.1 9.8 %convert_element_type.57 = f32[2,640,3,1024]{1,3,0,2:T(8,128)} convert(bf16[2,640,3,1024]{1,3,0,2:T(8,128)(2,1)} %all-reduce.2.cloned.1.call-done) | non-fusion elementwise | flops 3932160 | bytes 23592960 | tf_op jit(solution)/shard_map/convert_element_type | solution.py:65
  467.0 8.0 %multiply_convert_fusion.1 = (bf16[2,640,1024]{1,2,0:T(8,128)(2,1)}, bf16[2,640,1024]{1,2,0:T(8,128)(2,1)S(1)}) fusion(f32[2,640,3,1024]{1,3,0,2:T(8,128)} %convert_element_type.57), kind=kLoop, calls=%fused_computation.22 | loop fusion | flops 17039360 | bytes 20971520 | tf_op jit(solution)/shard_map/convert_element_type | solution.py:14
  475.0 11.8 %fusion.38 = f32[2,640,1792]{2,1,0:T(8,128)} fusion(bf16[2,640,1024]{1,2,0:T(8,128)(2,1)S(1)} %get-tuple-element.7, bf16[2,1792,1024]{2,1,0:T(8,128)(2,1)} %param.11), kind=kOutput, calls=%fused_computation.61 | convolution fusion | flops 4697620480 | bytes 19136512 | tf_op jit(solution)/shard_map/erf,edf->erd/dot_general | solution.py:79
  486.8 14.0 %add_convert_fusion = bf16[2,640,1792]{2,1,0:T(8,128)(2,1)} fusion(f32[2,640,1792]{2,1,0:T(8,128)} %fusion.38, bf16[2,640,1024]{1,2,0:T(8,128)(2,1)} %get-tuple-element.6, bf16[2,1792,1024]{2,1,0:T(8,128)(2,1)} %param.12), kind=kOutput, calls=%fused_computation.3 | convolution fusion | flops 4702208000 | bytes 23724032 | tf_op jit(solution)/shard_map/erf,edf->erd/dot_general | solution.py:80
  500.7 4.7 copy.73
  505.4 4.8 all-to-all-start.2
  510.3 2.6 copy.67
  512.9 2.7 copy.63
  516.1 9.5 %convolution_convert_fusion.1 = bf16[2,1792,1024]{2,1,0:T(8,128)(2,1)} fusion(bf16[2,640,1792]{2,1,0:T(8,128)(2,1)S(1)} %bitcast.101, bf16[2,640,1024]{1,2,0:T(8,128)(2,1)S(1)} %copy-done.2), kind=kOutput, calls=%fused_computation.16 | convolution fusion | flops 4701290496 | bytes 14548992 | tf_op jit(solution)/shard_map/erd,erf->edf/dot_general | solution.py:75
  525.5 9.4 %convolution_convert_fusion.2 = bf16[2,1792,1024]{2,1,0:T(8,128)(2,1)} fusion(bf16[2,640,1792]{2,1,0:T(8,128)(2,1)S(1)} %bitcast.102, bf16[2,640,1024]{1,2,0:T(8,128)(2,1)S(1)} %get-tuple-element.7), kind=kOutput, calls=%fused_computation.17 | convolution fusion | flops 4701290496 | bytes 14548992 | tf_op jit(solution)/shard_map/erd,erf->edf/dot_general | solution.py:72
  535.0 12.8 %convolution_convert_fusion = bf16[2,1024,1792]{2,1,0:T(8,128)(2,1)} fusion(bf16[2,640,1792]{2,1,0:T(8,128)(2,1)S(1)} %bitcast.100, f32[2,640,3,1024]{1,3,0,2:T(8,128)} %convert_element_type.57), kind=kOutput, calls=%fused_computation.15 | convolution fusion | flops 4709154816 | bytes 22413312 | tf_op jit(solution)/shard_map/erf,erd->efd/dot_general | solution.py:69
  547.8 15.8 %all-to-all-done.2 = bf16[2,8,80,1792]{3,2,0,1:T(8,128)(2,1)} async-done(((bf16[2,8,80,1792]{3,2,0,1:T(8,128)(2,1)}), bf16[2,8,80,1792]{3,2,0,1:T(8,128)(2,1)}, u32[]{:S(2)}, u32[]{:S(2)}) %all-to-all-start.2) | async-done | bytes 4587552 | tf_op jit(solution)/shard_map/all_to_all | solution.py:82
  563.6 4.6 copy.74
  568.2 10.9 %gather_fusion = bf16[1024,1792]{1,0:T(8,128)(2,1)} fusion(bf16[1280,1792]{1,0:T(8,128)(2,1)} %bitcast.97, s32[1024]{0:T(1024)S(1)} %broadcast_clamp_fusion), kind=kCustom, calls=%fused_computation | custom fusion | bytes 7344128 | tf_op jit(solution)/shard_map/gather | solution.py:92
  579.1 6.3 %fusion = bf16[128,1792]{1,0:T(8,128)(2,1)} fusion(bf16[1024,1792]{1,0:T(8,128)(2,1)} %gather_fusion, pred[128,8]{1,0:T(8,128)(4,1)S(1)} %lt.50), kind=kLoop, calls=%fused_computation.6 | loop fusion | flops 5275648 | bytes 4129792 | tf_op jit(solution)/shard_map/reduce_sum | solution.py:94
  (28 shorter events, 4.1 us)
Async XLA Ops:
  7.2 27.2 %copy-start = (bf16[128,1792]{1,0:T(8,128)(2,1)S(1)}, bf16[128,1792]{1,0:T(8,128)(2,1)}, u32[]{:S(2)}) copy-start(bf16[128,1792]{1,0:T(8,128)(2,1)} %param.7) | copy-start | bytes 1376260
  29.2 58.6 %all-to-all-start.1 = ((bf16[2,8,80,1792]{3,2,0,1:T(8,128)(2,1)}), bf16[2,8,80,1792]{3,2,0,1:T(8,128)(2,1)}, u32[]{:S(2)}, u32[]{:S(2)}) async-start(bf16[2,8,80,1792]{3,2,0,1:T(8,128)(2,1)} %copy.66), calls=%async_computation.1 | async-start | bytes 9175040 | tf_op jit(solution)/shard_map/all_to_all | solution.py:54
  87.8 58.4 %all-to-all-start = ((bf16[2,8,80,1792]{3,2,0,1:T(8,128)(2,1)}), bf16[2,8,80,1792]{3,2,0,1:T(8,128)(2,1)}, u32[]{:S(2)}, u32[]{:S(2)}) async-start(bf16[2,8,80,1792]{3,2,0,1:T(8,128)(2,1)} %copy.62), calls=%async_computation | async-start | bytes 9175040 | tf_op jit(solution)/shard_map/all_to_all | solution.py:53
  92.9 364.2 %all-reduce.2.cloned.1.call-start = ((), (), s32[]{:S(2)}) async-start(), calls=%async_computation.3 | async-start | bytes 15728640 | tf_op jit(solution)/shard_map/psum | solution.py:65
  505.4 58.1 %all-to-all-start.2 = ((bf16[2,8,80,1792]{3,2,0,1:T(8,128)(2,1)}), bf16[2,8,80,1792]{3,2,0,1:T(8,128)(2,1)}, u32[]{:S(2)}, u32[]{:S(2)}) async-start(bf16[2,8,80,1792]{3,2,0,1:T(8,128)(2,1)} %copy.73), calls=%async_computation.2 | async-start | bytes 9175040 | tf_op jit(solution)/shard_map/all_to_all | solution.py:82
  512.9 3.1 copy-start.2
  568.2 17.1 %copy-start.1 = (bf16[128,1792]{1,0:T(8,128)(2,1)S(1)}, bf16[128,1792]{1,0:T(8,128)(2,1)}, u32[]{:S(2)}) copy-start(bf16[128,1792]{1,0:T(8,128)(2,1)} %param.7) | copy-start | bytes 1376260
Sparse Core Ops, SparseCore 0:
  183.2 273.9 all-reduce.1
where the time goes:
time: 602 us; the launch traced here: 593 us
  waiting for transfers between devices  369 us (61%)
  matrix products  90.1 us (15%)
  local copies, waits for them, and re-layouts  58.5 us (10%)
  other arithmetic  45.3 us (8%)
  starting transfers between devices  15.1 us (3%)
  between operations  14.6 us (2%)
    psum x1, waiting for transfers between devices, on_device(): totals = lax.psum(stacked.astype(jnp.bfloat16), 'local').astype(jnp.float32)  274 us
    all_to_all x1, waiting for transfers between devices, on_device(): lax.all_to_all(dy_send, 'node', split_axis=1, concat_axis=1, tiled=True)  39.9 us
    all_to_all x1, waiting for transfers between devices, on_device(): lax.all_to_all(x_send, 'node', split_axis=1, concat_axis=1, tiled=True)  39.2 us
    all_to_all x1, waiting for transfers between devices, on_device(): lax.all_to_all(grad_rows.reshape(exp_local, node_count, capacity, slice_w...  15.8 us
    dot_general x1, matrix products, on_device(): jnp.einsum('erf,edf->erd', grad_up, up_weight, preferred_element_type=jnp...  14 us
    dot_general x1, matrix products, on_device(): jnp.einsum('erf,erd->efd', hidden_act, dy_flat, preferred_element_type=jn...  12.8 us
  transfers between devices with their start and end apart: 4, of which 4 were waited for; matrix products, arithmetic and copies ran while one was open for 11% of the time, Pallas kernels for 0%

commit v1 on v0

v1 whole, which is shorter than its diff:
```python
import functools

import jax
import jax.numpy as jnp
from jax import lax
from jax.experimental import pallas as pl
from jax.experimental.pallas import tpu as pltpu
from jax.sharding import PartitionSpec as P

MESH = pl.DeviceIdType.MESH


def swiglu_backward(gate_pre, up_pre, grad_hidden):
    sigmoid_g = jax.nn.sigmoid(gate_pre)
    activated = gate_pre * sigmoid_g
    hidden_act = (activated * up_pre).astype(jnp.bfloat16)
    grad_gate = (grad_hidden * up_pre * sigmoid_g * (1.0 + gate_pre * (1.0 - sigmoid_g))).astype(
        jnp.bfloat16
    )
    grad_up = (grad_hidden * activated).astype(jnp.bfloat16)
    return (hidden_act, grad_gate, grad_up)


def width_sum_kernel(
    n, chunks, ch, hop,
    g_ref, u_ref, h_ref, act_ref, gg_ref, gu_ref,
    part, done, part_send, part_recv, done_send, done_recv,
):
    me = lax.axis_index("local")
    half = chunks * ch
    ins = (g_ref, u_ref, h_ref)
    outs = (act_ref, gg_ref, gu_ref)

    barrier = pltpu.get_barrier_semaphore()

    @pl.when(me > 0)
    def _():
        pl.semaphore_signal(barrier, inc=1, device_id={"local": me - 1}, device_id_type=MESH)

    @pl.when(me < n - 1)
    def _():
        pl.semaphore_signal(barrier, inc=1, device_id={"local": me + 1}, device_id_type=MESH)

    pl.semaphore_wait(barrier, (me > 0).astype(jnp.int32) + (me < n - 1).astype(jnp.int32))

    def part_copy(way, c):
        target = me - 1 if way == 0 else me + 1
        return pltpu.make_async_remote_copy(
            src_ref=part.at[way, c],
            dst_ref=part.at[way, c],
            send_sem=part_send.at[way, c],
            recv_sem=part_recv.at[way, c],
            device_id={"local": target},
            device_id_type=MESH,
        )

    def done_copy(way, c):
        target = me + 1 if way == 0 else me - 1
        return pltpu.make_async_remote_copy(
            src_ref=done.at[way, c],
            dst_ref=done.at[way, c],
            send_sem=done_send.at[way, c],
            recv_sem=done_recv.at[way, c],
            device_id={"local": target},
            device_id_type=MESH,
        )

    def rows_of(way, c):
        return pl.ds(pl.multiple_of(way * half + c * ch, ch), ch)

    def step(s, carry):
        for way in range(2):
            dist = me if way == 0 else n - 1 - me
            c = s - hop * (n - 1 - dist)
            live = jnp.logical_and(c >= 0, c < chunks)

            @pl.when(jnp.logical_and(live, dist == n - 1))
            def _():
                rows = rows_of(way, c)
                for j in range(3):
                    part[way, c, pl.ds(j * ch, ch), :] = ins[j][rows, :]
                part_copy(way, c).start()

            @pl.when(jnp.logical_and(live, jnp.logical_and(dist > 0, dist < n - 1)))
            def _():
                part_copy(way, c).wait_recv()
                rows = rows_of(way, c)
                for j in range(3):
                    at = pl.ds(j * ch, ch)
                    total = part[way, c, at, :].astype(jnp.float32) + ins[j][rows, :].astype(
                        jnp.float32
                    )
                    part[way, c, at, :] = total.astype(jnp.bfloat16)
                part_copy(way, c).start()

            @pl.when(jnp.logical_and(live, dist == 0))
            def _():
                part_copy(way, c).wait_recv()
                rows = rows_of(way, c)
                sums = [
                    part[way, c, pl.ds(j * ch, ch), :].astype(jnp.float32)
                    + ins[j][rows, :].astype(jnp.float32)
                    for j in range(3)
                ]
                for j, value in enumerate(swiglu_backward(*sums)):
                    done[way, c, pl.ds(j * ch, ch), :] = value
                    outs[j][rows, :] = value
                done_copy(way, c).start()

            k = s - hop * (n - 1) - hop * dist
            back = jnp.logical_and(jnp.logical_and(k >= 0, k < chunks), dist > 0)

            @pl.when(back)
            def _():
                done_copy(way, k).wait_recv()

            @pl.when(jnp.logical_and(back, dist < n - 1))
            def _():
                done_copy(way, k).start()

            @pl.when(back)
            def _():
                rows = rows_of(way, k)
                for j in range(3):
                    outs[j][rows, :] = done[way, k, pl.ds(j * ch, ch), :]

        return carry

    lax.fori_loop(0, chunks + 2 * hop * (n - 1), step, 0)

    def drain(c, carry):
        for way in range(2):
            dist = me if way == 0 else n - 1 - me

            @pl.when(dist > 0)
            def _():
                part_copy(way, c).wait_send()

            @pl.when(dist < n - 1)
            def _():
                done_copy(way, c).wait_send()

        return carry

    lax.fori_loop(0, chunks, drain, 0)


def width_sum(gate_pre, up_pre, grad_hidden):
    n = lax.axis_size("local")
    rows, hidden = gate_pre.shape
    half = rows // 2
    ch = 32 if half % 32 == 0 else 16
    chunks = half // ch
    shape = jax.ShapeDtypeStruct((rows, hidden), jnp.bfloat16)
    whole = pl.BlockSpec(memory_space=pltpu.VMEM)
    return pl.pallas_call(
        functools.partial(width_sum_kernel, n, chunks, ch, 2),
        out_shape=(shape, shape, shape),
        in_specs=[whole] * 3,
        out_specs=(whole, whole, whole),
        scratch_shapes=[
            pltpu.VMEM((2, chunks, 3 * ch, hidden), jnp.bfloat16),
            pltpu.VMEM((2, chunks, 3 * ch, hidden), jnp.bfloat16),
            pltpu.SemaphoreType.DMA((2, chunks)),
            pltpu.SemaphoreType.DMA((2, chunks)),
            pltpu.SemaphoreType.DMA((2, chunks)),
            pltpu.SemaphoreType.DMA((2, chunks)),
        ],
        compiler_params=pltpu.CompilerParams(
            collective_id=0, has_side_effects=True, vmem_limit_bytes=48 * 1024 * 1024
        ),
    )(gate_pre, up_pre, grad_hidden)


def on_device(tokens, out_grad, expert_ids, gates, gate_weight, up_weight, down_weight):
    tok_rows, slice_width = tokens.shape
    top_count = expert_ids.shape[1]
    node_count = lax.axis_size("node")
    exp_local = gate_weight.shape[0]
    hidden = gate_weight.shape[2]
    experts = exp_local * node_count
    capacity = tok_rows * top_count * 5 // (experts * 4)
    row_count = node_count * capacity

    routing = jnp.concatenate([expert_ids.astype(jnp.float32), gates], axis=1)
    routing = lax.all_gather(routing, "node")
    tok_all = lax.all_gather(tokens, "node")
    dy_all = lax.all_gather(out_grad, "node")

    ids_all = routing[:, :, :top_count].astype(jnp.int32)
    gates_all = routing[:, :, top_count:]
    mine = lax.axis_index("node") * exp_local + jnp.arange(exp_local, dtype=jnp.int32)
    hit = ids_all[None] == mine[:, None, None, None]
    named = jnp.any(hit, axis=3)
    gate_of = jnp.sum(jnp.where(hit, gates_all[None], 0.0), axis=3)
    before = jnp.arange(tok_rows)[:, None] < jnp.arange(tok_rows)[None, :]
    slot = jnp.einsum(
        "ebt,tu->ebu",
        named.astype(jnp.bfloat16),
        before.astype(jnp.bfloat16),
        preferred_element_type=jnp.float32,
    ).astype(jnp.int32)
    slot = jnp.where(named, slot, capacity)
    chosen = slot[:, :, None, :] == jnp.arange(capacity, dtype=jnp.int32)[None, None, :, None]
    gate_row = jnp.sum(jnp.where(chosen, gate_of[:, :, None, :], 0.0), axis=3)
    pick = chosen.astype(jnp.bfloat16)

    dy_rows = (
        jnp.einsum("ebst,btd->ebsd", pick, dy_all, preferred_element_type=jnp.float32)
        * gate_row[..., None]
    ).astype(jnp.bfloat16)
    x_rows = jnp.einsum(
        "ebst,btd->ebsd", pick, tok_all, preferred_element_type=jnp.float32
    ).astype(jnp.bfloat16)
    x_flat = x_rows.reshape(exp_local, row_count, slice_width)
    dy_flat = dy_rows.reshape(exp_local, row_count, slice_width)

    def partial(spec, rows, weight):
        value = jnp.einsum(spec, rows, weight, preferred_element_type=jnp.float32)
        return value.astype(jnp.bfloat16).reshape(exp_local * row_count, hidden)

    gate_pre = partial("erd,edf->erf", x_flat, gate_weight)
    up_pre = partial("erd,edf->erf", x_flat, up_weight)
    grad_hidden = partial("erd,efd->erf", dy_flat, down_weight)
    hidden_act, grad_gate, grad_up = (
        v.reshape(exp_local, row_count, hidden) for v in width_sum(gate_pre, up_pre, grad_hidden)
    )

    grad_rows = (
        jnp.einsum("erf,edf->erd", grad_gate, gate_weight, preferred_element_type=jnp.float32)
        + jnp.einsum("erf,edf->erd", grad_up, up_weight, preferred_element_type=jnp.float32)
    ).astype(jnp.bfloat16)
    back = jnp.einsum(
        "ebst,ebsd->btd",
        pick,
        grad_rows.reshape(exp_local, node_count, capacity, slice_width),
        preferred_element_type=jnp.float32,
    ).astype(jnp.bfloat16)
    grad_tokens = lax.psum_scatter(back, "node", scatter_dimension=0, tiled=False)

    down_grad = jnp.einsum(
        "erf,erd->efd", hidden_act, dy_flat, preferred_element_type=jnp.float32
    ).astype(jnp.bfloat16)
    gate_grad = jnp.einsum(
        "erd,erf->edf", x_flat, grad_gate, preferred_element_type=jnp.float32
    ).astype(jnp.bfloat16)
    up_grad = jnp.einsum(
        "erd,erf->edf", x_flat, grad_up, preferred_element_type=jnp.float32
    ).astype(jnp.bfloat16)
    return (grad_tokens, gate_grad, up_grad, down_grad)


def solution(mesh):
    return jax.shard_map(
        on_device,
        mesh=mesh,
        in_specs=(
            P("node", "local"),
            P("node", "local"),
            P("node", None),
            P("node", None),
            P("node", "local", None),
            P("node", "local", None),
            P("node", None, "local"),
        ),
        out_specs=(
            P("node", "local"),
            P("node", "local", None),
            P("node", "local", None),
            P("node", None, "local"),
        ),
        check_vma=False,
    )
```

time: 602 us -> 397 us (0.66); the launches traced: 593 us -> 397 us
  waiting for transfers between devices: 369 us -> 76 us
  Pallas kernels: 0 us -> 201 us
  local copies, waits for them, and re-layouts: 58.5 us -> 2.85 us
  other arithmetic: 45.3 us -> 1.96 us
  starting transfers between devices: 15.1 us -> 0.11 us
  blocking collectives: 0 us -> 10.5 us
    psum x1 -> x0, waiting for transfers between devices: 274 us -> none  [on_device(): totals = lax.psum(stacked.astype(jnp.bfloat16), 'local').astype(jnp.float32)]
    pallas_call x0 -> x1, Pallas kernels: none -> 201 us  [width_sum(): pl.pallas_call(functools.partial(width_sum_kernel, n, chunks, ch, 2), out...]
    all_to_all x3 -> x0, waiting for transfers between devices: 94.9 us -> none  [the longest x1 39.9 us: on_device(): lax.all_to_all(dy_send, 'node', split_axis=1, concat_axis=1, tiled=True)]
    all_gather x0 -> x2, waiting for transfers between devices: none -> 56.3 us  [the longest x1 30.6 us: on_device(): tok_all = lax.all_gather(tokens, 'node')]
    reduce_scatter x0 -> x1, waiting for transfers between devices: none -> 18.3 us  [on_device(): lax.psum_scatter(back, 'node', scatter_dimension=0, tiled=False)]
    convert_element_type x4 -> x1, other arithmetic: 18.9 us -> 0.69 us  [on_device(): routing = jnp.concatenate([expert_ids.astype(jnp.float32), gates], axis=1)]
    all_to_all x3 -> x0, starting transfers between devices: 15 us -> none  [the longest x1 5.17 us: on_device(): lax.all_to_all(dy_send, 'node', split_axis=1, concat_axis=1, tiled=True)]
    reshape x4 -> x0, local copies, waits for them, and re-layouts: 14.3 us -> none  [the longest x1 4.77 us: on_device(): x_send = blank.at[dest_row].set(x_rep, mode='drop').reshape(exp_local, no...]
  transfers between devices with their start and end apart: 4 -> 3, of which waited for: 4 -> 3; matrix products, arithmetic and copies ran while one was open for 11% -> 10% of each run, Pallas kernels for 0% -> 0%
where the time goes in v1:
time: 397 us
  Pallas kernels  201 us (51%)
  matrix products  90.5 us (23%)
  waiting for transfers between devices  76 us (19%)
  between operations  14 us (4%)
  blocking collectives  10.5 us (3%)
    pallas_call x1, Pallas kernels, width_sum(): pl.pallas_call(functools.partial(width_sum_kernel, n, chunks, ch, 2), out...  201 us
    all_gather x1, waiting for transfers between devices, on_device(): tok_all = lax.all_gather(tokens, 'node')  30.6 us
    all_gather x1, waiting for transfers between devices, on_device(): dy_all = lax.all_gather(out_grad, 'node')  25.7 us
    dot_general x3, matrix products, partial(): value = jnp.einsum(spec, rows, weight, preferred_element_type=jnp.float32)  23.6 us
    reduce_scatter x1, waiting for transfers between devices, on_device(): lax.psum_scatter(back, 'node', scatter_dimension=0, tiled=False)  18.3 us
    dot_general x1, matrix products, on_device(): jnp.einsum('erf,edf->erd', grad_up, up_weight, preferred_element_type=jnp...  13.7 us
    dot_general x1, matrix products, on_device(): jnp.einsum('erf,edf->erd', grad_gate, gate_weight, preferred_element_type...  11.4 us
    dot_general x1, matrix products, on_device(): jnp.einsum('erd,erf->edf', x_flat, grad_up, preferred_element_type=jnp.fl...  10.8 us
  transfers between devices with their start and end apart: 3, of which 3 were waited for; matrix products, arithmetic and copies ran while one was open for 10% of the time, Pallas kernels for 0%

profile of v1, /device:TPU:0, one launch (start us, length us, event | category | flops | bytes accessed | tf_op | source)
XLA Modules:
  0.0 396.6 jit_solution(14022336330143767045)
XLA Ops:
  7.2 0.0 all-gather.8.cloned.1.call-start
  7.2 0.7 all-gather.8.cloned.1.call-update
  7.9 0.0 all-gather.6.cloned.1.call-start
  7.9 0.7 all-gather.6.cloned.1.call-update
  8.6 0.0 reduce-scatter.2.cloned.1.call-start
  8.7 0.7 convert_element_type.45
  9.4 0.7 pad_maximum_fusion
  10.1 10.5 %all-gather = f32[1024,16]{0,1:T(8,128)S(1)} all-gather(f32[128,16]{0,1:T(8,128)S(1)} %pad_maximum_fusion), channel_id=2, replica_groups=mesh['node'=8,'local'=4] {'node'}, dimensions={0}, use_global_device_ids=true | all-gather | bytes 73728 | tf_op jit(solution)/shard_map/all_gather | solution.py:186
  20.7 0.1 compare_reduce_fusion
  20.8 0.1 fusion.5
  20.9 0.1 fusion.9
  21.0 0.4 select_reduce_fusion
  21.4 25.7 %all-gather.8.cloned.1.call-done = bf16[1024,1792]{1,0:T(8,128)(2,1)} async-done(((bf16[128,1792]{1,0:T(8,128)(2,1)}), bf16[1024,1792]{1,0:T(8,128)(2,1)}) %all-gather.8.cloned.1.call-update) | async-done | bytes 3670032 | tf_op jit(solution)/shard_map/all_gather | solution.py:188
  47.1 3.4 fusion
  50.5 2.4 copy.32
  53.0 30.6 %all-gather.6.cloned.1.call-done = bf16[1024,1792]{1,0:T(8,128)(2,1)} async-done(((bf16[128,1792]{1,0:T(8,128)(2,1)}), bf16[1024,1792]{1,0:T(8,128)(2,1)}) %all-gather.6.cloned.1.call-update) | async-done | bytes 3670032 | tf_op jit(solution)/shard_map/all_gather | solution.py:187
  83.6 3.4 convert_bitcast_fusion
  86.9 0.0 slice-start.6
  87.0 0.3 copy.29
  87.3 11.2 %convolution_convert_fusion.5 = bf16[2,640,1024]{2,1,0:T(8,128)(2,1)} fusion(bf16[2,640,1792]{2,1,0:T(8,128)(2,1)S(1)} %bitcast.66, bf16[2,1792,1024]{2,1,0:T(8,128)(2,1)} %param.11), kind=kOutput, calls=%fused_computation.12 | convolution fusion | flops 4698931200 | bytes 14548992 | tf_op jit(solution)/shard_map/erd,edf->erf/dot_general | solution.py:219
  98.5 0.0 slice-start.5
  98.6 6.2 %convolution_convert_fusion.4 = bf16[2,640,1024]{2,1,0:T(8,128)(2,1)} fusion(bf16[2,640,1792]{2,1,0:T(8,128)(2,1)S(1)} %bitcast.67, bf16[2,1792,1024]{2,1,0:T(8,128)(2,1)S(1)} %bitcast.79), kind=kOutput, calls=%fused_computation.11 | convolution fusion | flops 4698931200 | bytes 14548992 | tf_op jit(solution)/shard_map/erd,edf->erf/dot_general | solution.py:219
  104.8 6.2 %convolution_convert_fusion.3 = bf16[2,640,1024]{2,1,0:T(8,128)(2,1)} fusion(bf16[2,640,1792]{2,1,0:T(8,128)(2,1)S(1)} %bitcast.62, bf16[2,1024,1792]{2,1,0:T(8,128)(2,1)S(1)} %bitcast.77), kind=kOutput, calls=%fused_computation.10 | convolution fusion | flops 4698931200 | bytes 14548992 | tf_op jit(solution)/shard_map/erd,efd->erf/dot_general | solution.py:219
  111.0 200.7 %shard_map.102 = (bf16[1280,1024]{1,0:T(8,128)(2,1)S(1)}, bf16[1280,1024]{1,0:T(8,128)(2,1)S(1)}, bf16[1280,1024]{1,0:T(8,128)(2,1)}) custom-call(bf16[1280,1024]{1,0:T(8,128)(2,1)} %bitcast.71, bf16[1280,1024]{1,0:T(8,128)(2,1)} %bitcast.72, bf16[1280,1024]{1,0:T(8,128)(2,1)} %bitcast.73), custom_call_target="tpu_custom_call" | custom-call | tf_op jit(solution)/shard_map/pallas_call | solution.py:156
  311.7 11.4 %fusion.13 = f32[2,640,1792]{2,1,0:T(8,128)} fusion(bf16[2,640,1024]{2,1,0:T(8,128)(2,1)S(1)} %bitcast.56, bf16[2,1792,1024]{2,1,0:T(8,128)(2,1)} %param.11), kind=kOutput, calls=%fused_computation.29 | convolution fusion | flops 4697620480 | bytes 19136512 | tf_op jit(solution)/shard_map/erf,edf->erd/dot_general | solution.py:230
  323.1 13.7 %add_convert_fusion = bf16[2,640,1792]{2,1,0:T(8,128)(2,1)} fusion(f32[2,640,1792]{2,1,0:T(8,128)} %fusion.13, bf16[2,640,1024]{2,1,0:T(8,128)(2,1)} %bitcast.80, bf16[2,1792,1024]{2,1,0:T(8,128)(2,1)} %param.12), kind=kOutput, calls=%fused_computation.2 | convolution fusion | flops 4702208000 | bytes 23724032 | tf_op jit(solution)/shard_map/erf,edf->erd/dot_general | solution.py:231
  336.8 5.2 %bitcast_convert_fusion = bf16[8,128,1792]{2,1,0:T(8,128)(2,1)} fusion(bf16[2,8,80,1792]{3,2,1,0:T(8,128)(2,1)} %bitcast.70, s32[2,8,128]{2,0,1:T(2,128)S(1)} %copy.28), kind=kOutput, calls=%fused_computation.3 | convolution fusion | flops 589201408 | bytes 8265728 | tf_op jit(solution)/shard_map/ebst,ebsd->btd/dot_general | solution.py:233
  342.1 0.0 reduce-scatter.2.cloned.1.call-update
  342.1 10.8 %convolution_convert_fusion.1 = bf16[2,1792,1024]{2,1,0:T(8,128)(2,1)} fusion(bf16[2,640,1792]{2,1,0:T(8,128)(2,1)} %bitcast.68, bf16[2,640,1024]{2,1,0:T(8,128)(2,1)} %bitcast.81), kind=kOutput, calls=%fused_computation.5 | convolution fusion | flops 4701290496 | bytes 14548992 | tf_op jit(solution)/shard_map/erd,erf->edf/dot_general | solution.py:247
  352.9 10.7 %convolution_convert_fusion.2 = bf16[2,1792,1024]{2,1,0:T(8,128)(2,1)} fusion(bf16[2,640,1792]{2,1,0:T(8,128)(2,1)} %bitcast.69, bf16[2,640,1024]{2,1,0:T(8,128)(2,1)S(1)} %bitcast.57), kind=kOutput, calls=%fused_computation.6 | convolution fusion | flops 4701290496 | bytes 14548992 | tf_op jit(solution)/shard_map/erd,erf->edf/dot_general | solution.py:244
  363.7 8.2 %convolution_convert_fusion = bf16[2,1024,1792]{2,1,0:T(8,128)(2,1)} fusion(bf16[2,640,1024]{2,1,0:T(8,128)(2,1)S(1)} %bitcast.55, bf16[2,640,1792]{2,1,0:T(8,128)(2,1)S(1)} %bitcast.65), kind=kOutput, calls=%fused_computation.4 | convolution fusion | flops 4701290496 | bytes 14548992 | tf_op jit(solution)/shard_map/erf,erd->efd/dot_general | solution.py:241
  371.8 18.3 %reduce-scatter.2.cloned.1.call-done = bf16[1,128,1792]{2,1,0:T(8,128)(2,1)} async-done(((bf16[8,128,1792]{2,1,0:T(8,128)(2,1)}), bf16[1,128,1792]{2,1,0:T(8,128)(2,1)}) %reduce-scatter.2.cloned.1.call-update) | async-done | bytes 458768 | tf_op jit(solution)/shard_map/reduce_scatter | solution.py:239
  (31 shorter events, 0.1 us)
Async XLA Ops:
  7.2 40.0 %all-gather.8.cloned.1.call-start = ((), (), s32[]{:S(2)}) async-start(), calls=%async_computation.3 | async-start | bytes 4128768 | tf_op jit(solution)/shard_map/all_gather | solution.py:188
  7.9 75.7 %all-gather.6.cloned.1.call-start = ((), (), s32[]{:S(2)}) async-start(), calls=%async_computation.2 | async-start | bytes 4128768 | tf_op jit(solution)/shard_map/all_gather | solution.py:187
  8.6 381.5 %reduce-scatter.2.cloned.1.call-start = ((), (), s32[]{:S(2)}) async-start(), calls=%async_computation.1 | async-start | bytes 4128768 | tf_op jit(solution)/shard_map/reduce_scatter | solution.py:239
  86.9 11.6 %slice-start.6 = ((s8[7340032]{0:T(1024)(128)(4,1)}), s8[3145728]{0:T(1024)(128)(4,1)S(1)}, s32[]{:S(2)}) async-start(s8[7340032]{0:T(1024)(128)(4,1)} %bitcast.78), calls=%async_computation.10 | async-start | bytes 6291456
  87.3 11.3 %copy-start.2 = (bf16[2,8,80,1792]{3,2,1,0:T(8,128)(2,1)}, bf16[2,8,80,1792]{3,2,1,0:T(8,128)(2,1)S(1)}, u32[]{:S(2)}) copy-start(bf16[2,8,80,1792]{3,2,1,0:T(8,128)(2,1)S(1)} %copy.29) | copy-start | bytes 13762564
  87.3 11.3 %slice-start.7 = ((s8[7340032]{0:T(1024)(128)(4,1)}), s8[4194304]{0:T(1024)(128)(4,1)S(1)}, s32[]{:S(2)}) async-start(s8[7340032]{0:T(1024)(128)(4,1)} %bitcast.78), calls=%async_computation.11 | async-start | bytes 8388608
  87.3 17.4 %slice-start = ((s8[4587520]{0:T(1024)(128)(4,1)}), s8[4194304]{0:T(1024)(128)(4,1)S(1)}, s32[]{:S(2)}) async-start(s8[4587520]{0:T(1024)(128)(4,1)} %bitcast.60), calls=%async_computation.4 | async-start | bytes 8388608
  87.3 17.4 %slice-start.4 = ((s8[7340032]{0:T(1024)(128)(4,1)}), s8[4194304]{0:T(1024)(128)(4,1)S(1)}, s32[]{:S(2)}) async-start(s8[7340032]{0:T(1024)(128)(4,1)} %bitcast.76), calls=%async_computation.8 | async-start | bytes 8388608
  98.5 6.2 %slice-start.1 = ((s8[4587520]{0:T(1024)(128)(4,1)}), s8[393216]{0:T(1024)(128)(4,1)S(1)}, s32[]{:S(2)}) async-start(s8[4587520]{0:T(1024)(128)(4,1)} %bitcast.60), calls=%async_computation.5 | async-start | bytes 786432
  98.5 6.2 %slice-start.5 = ((s8[7340032]{0:T(1024)(128)(4,1)}), s8[3145728]{0:T(1024)(128)(4,1)S(1)}, s32[]{:S(2)}) async-start(s8[7340032]{0:T(1024)(128)(4,1)} %bitcast.76), calls=%async_computation.9 | async-start | bytes 6291456
  311.7 11.4 %copy-start = (bf16[1280,1024]{1,0:T(8,128)(2,1)}, bf16[1280,1024]{1,0:T(8,128)(2,1)S(1)}, u32[]{:S(2)}) copy-start(bf16[1280,1024]{1,0:T(8,128)(2,1)S(1)} %get-tuple-element.7) | copy-start | bytes 7864324
  342.1 10.9 %copy-start.1 = (bf16[1280,1024]{1,0:T(8,128)(2,1)S(1)}, bf16[1280,1024]{1,0:T(8,128)(2,1)}, u32[]{:S(2)}) copy-start(bf16[1280,1024]{1,0:T(8,128)(2,1)} %copy-done) | copy-start | bytes 7864324
  342.1 21.6 %slice-start.2 = ((s8[4587520]{0:T(1024)(128)(4,1)}), s8[4194304]{0:T(1024)(128)(4,1)S(1)}, s32[]{:S(2)}) async-start(s8[4587520]{0:T(1024)(128)(4,1)} %bitcast.63), calls=%async_computation.6 | async-start | bytes 8388608
  352.9 10.7 %slice-start.3 = ((s8[4587520]{0:T(1024)(128)(4,1)}), s8[393216]{0:T(1024)(128)(4,1)S(1)}, s32[]{:S(2)}) async-start(s8[4587520]{0:T(1024)(128)(4,1)} %bitcast.63), calls=%async_computation.7 | async-start | bytes 786432
Sparse Core Ops, SparseCore 0:
  9.9 37.2 all-gather.7
  49.0 34.5 all-gather.5
  342.2 47.8 reduce-scatter.1

commit v2 on v1

--- a/solution.py
+++ b/solution.py
@@ -22,14 +22,19 @@
 
 
 def width_sum_kernel(
-    n, chunks, ch, hop,
-    g_ref, u_ref, h_ref, act_ref, gg_ref, gu_ref,
-    part, done, part_send, part_recv, done_send, done_recv,
+    n, chunks, ch, hop, block, expert_rows,
+    g_ref, u_ref, h_ref, gw_ref, uw_ref, act_ref, gg_ref, gu_ref, row_ref,
+    part, done, gw, uw, part_send, part_recv, done_send, done_recv, weight_sem,
 ):
     me = lax.axis_index("local")
     half = chunks * ch
     ins = (g_ref, u_ref, h_ref)
     outs = (act_ref, gg_ref, gu_ref)
+
+    gw_copy = pltpu.make_async_copy(gw_ref, gw, weight_sem.at[0])
+    uw_copy = pltpu.make_async_copy(uw_ref, uw, weight_sem.at[1])
+    gw_copy.start()
+    uw_copy.start()
 
     barrier = pltpu.get_barrier_semaphore()
 
@@ -67,6 +72,26 @@
 
     def rows_of(way, c):
         return pl.ds(pl.multiple_of(way * half + c * ch, ch), ch)
+
+    def row_block(way, b):
+        start = way * half + b * block
+        expert = start // expert_rows
+        rows = pl.ds(pl.multiple_of(start, block), block)
+        dims = (((1,), (1,)), ((), ()))
+        width = gw.shape[1]
+        tile = 256 if width % 256 == 0 else 128
+
+        def columns(j, carry):
+            at = pl.ds(pl.multiple_of(j * tile, tile), tile)
+            total = lax.dot_general(
+                gg_ref[rows, :], gw[expert, at, :], dims, preferred_element_type=jnp.float32
+            ) + lax.dot_general(
+                gu_ref[rows, :], uw[expert, at, :], dims, preferred_element_type=jnp.float32
+            )
+            row_ref[rows, at] = total.astype(jnp.bfloat16)
+            return carry
+
+        lax.fori_loop(0, width // tile, columns, 0)
 
     def step(s, carry):
         for way in range(2):
@@ -124,9 +149,22 @@
                 for j in range(3):
                     outs[j][rows, :] = done[way, k, pl.ds(j * ch, ch), :]
 
+        for way in range(2):
+            dist = me if way == 0 else n - 1 - me
+            k = s - hop * (n - 1) - hop * dist
+            ready = jnp.logical_and(k >= 0, k < chunks)
+            full = (k + 1) * ch % block == 0
+
+            @pl.when(jnp.logical_and(ready, full))
+            def _():
+                row_block(way, k * ch // block)
+
         return carry
 
-    lax.fori_loop(0, chunks + 2 * hop * (n - 1), step, 0)
+    lax.fori_loop(0, hop * (n - 1), step, 0)
+    gw_copy.wait()
+    uw_copy.wait()
+    lax.fori_loop(hop * (n - 1), chunks + 2 * hop * (n - 1), step, 0)
 
     def drain(c, carry):
         for way in range(2):
@@ -145,31 +183,39 @@
     lax.fori_loop(0, chunks, drain, 0)
 
 
-def width_sum(gate_pre, up_pre, grad_hidden):
+def width_sum(gate_pre, up_pre, grad_hidden, gate_weight, up_weight):
     n = lax.axis_size("local")
     rows, hidden = gate_pre.shape
     half = rows // 2
-    ch = 32 if half % 32 == 0 else 16
+    ch = 16
+    expert_rows = rows // gate_weight.shape[0]
+    block = 128 if half % 128 == 0 and expert_rows % 128 == 0 else ch
     chunks = half // ch
     shape = jax.ShapeDtypeStruct((rows, hidden), jnp.bfloat16)
     whole = pl.BlockSpec(memory_space=pltpu.VMEM)
     return pl.pallas_call(
-        functools.partial(width_sum_kernel, n, chunks, ch, 2),
-        out_shape=(shape, shape, shape),
-        in_specs=[whole] * 3,
-        out_specs=(whole, whole, whole),
+        functools.partial(width_sum_kernel, n, chunks, ch, 2, block, expert_rows),
+        out_shape=(
+            shape, shape, shape,
+            jax.ShapeDtypeStruct((rows, gate_weight.shape[1]), jnp.bfloat16),
+        ),
+        in_specs=[whole] * 3 + [pl.BlockSpec(memory_space=pl.ANY)] * 2,
+        out_specs=(whole, whole, whole, whole),
         scratch_shapes=[
             pltpu.VMEM((2, chunks, 3 * ch, hidden), jnp.bfloat16),
             pltpu.VMEM((2, chunks, 3 * ch, hidden), jnp.bfloat16),
+            pltpu.VMEM(gate_weight.shape, jnp.bfloat16),
+            pltpu.VMEM(up_weight.shape, jnp.bfloat16),
             pltpu.SemaphoreType.DMA((2, chunks)),
             pltpu.SemaphoreType.DMA((2, chunks)),
             pltpu.SemaphoreType.DMA((2, chunks)),
             pltpu.SemaphoreType.DMA((2, chunks)),
+            pltpu.SemaphoreType.DMA((2,)),
         ],
         compiler_params=pltpu.CompilerParams(
-            collective_id=0, has_side_effects=True, vmem_limit_bytes=48 * 1024 * 1024
+            collective_id=0, has_side_effects=True, vmem_limit_bytes=60 * 1024 * 1024
         ),
-    )(gate_pre, up_pre, grad_hidden)
+    )(gate_pre, up_pre, grad_hidden, gate_weight, up_weight)
 
 
 def on_device(tokens, out_grad, expert_ids, gates, gate_weight, up_weight, down_weight):
@@ -185,6 +231,7 @@
     routing = jnp.concatenate([expert_ids.astype(jnp.float32), gates], axis=1)
     routing = lax.all_gather(routing, "node")
     tok_all = lax.all_gather(tokens, "node")
+    routing, out_grad = lax.optimization_barrier((routing, out_grad))
     dy_all = lax.all_gather(out_grad, "node")
 
     ids_all = routing[:, :, :top_count].astype(jnp.int32)
@@ -205,31 +252,31 @@
     gate_row = jnp.sum(jnp.where(chosen, gate_of[:, :, None, :], 0.0), axis=3)
     pick = chosen.astype(jnp.bfloat16)
 
-    dy_rows = (
-        jnp.einsum("ebst,btd->ebsd", pick, dy_all, preferred_element_type=jnp.float32)
-        * gate_row[..., None]
-    ).astype(jnp.bfloat16)
-    x_rows = jnp.einsum(
-        "ebst,btd->ebsd", pick, tok_all, preferred_element_type=jnp.float32
-    ).astype(jnp.bfloat16)
-    x_flat = x_rows.reshape(exp_local, row_count, slice_width)
-    dy_flat = dy_rows.reshape(exp_local, row_count, slice_width)
-
     def partial(spec, rows, weight):
         value = jnp.einsum(spec, rows, weight, preferred_element_type=jnp.float32)
         return value.astype(jnp.bfloat16).reshape(exp_local * row_count, hidden)
 
+    x_flat = (
+        jnp.einsum("ebst,btd->ebsd", pick, tok_all, preferred_element_type=jnp.float32)
+        .astype(jnp.bfloat16)
+        .reshape(exp_local, row_count, slice_width)
+    )
     gate_pre = partial("erd,edf->erf", x_flat, gate_weight)
     up_pre = partial("erd,edf->erf", x_flat, up_weight)
+    gate_pre, up_pre, dy_all = lax.optimization_barrier((gate_pre, up_pre, dy_all))
+    dy_flat = (
+        (
+            jnp.einsum("ebst,btd->ebsd", pick, dy_all, preferred_element_type=jnp.float32)
+            * gate_row[..., None]
+        )
+        .astype(jnp.bfloat16)
+        .reshape(exp_local, row_count, slice_width)
+    )
     grad_hidden = partial("erd,efd->erf", dy_flat, down_weight)
-    hidden_act, grad_gate, grad_up = (
-        v.reshape(exp_local, row_count, hidden) for v in width_sum(gate_pre, up_pre, grad_hidden)
-    )
-
-    grad_rows = (
-        jnp.einsum("erf,edf->erd", grad_gate, gate_weight, preferred_element_type=jnp.float32)
-        + jnp.einsum("erf,edf->erd", grad_up, up_weight, preferred_element_type=jnp.float32)
-    ).astype(jnp.bfloat16)
+    hidden_act, grad_gate, grad_up, grad_rows = (
+        v.reshape(exp_local, row_count, -1)
+        for v in width_sum(gate_pre, up_pre, grad_hidden, gate_weight, up_weight)
+    )
     back = jnp.einsum(
         "ebst,ebsd->btd",
         pick,

time: 397 us -> 358 us (0.902)
  matrix products: 90.5 us -> 57.8 us
  waiting for transfers between devices: 76 us -> 69 us
    dot_general x2 -> x0, matrix products: 25.1 us -> none  [the longest x1 13.7 us: on_device(): jnp.einsum('erf,edf->erd', grad_up, up_weight, preferred_element_type=jnp...]
    all_gather x1, waiting for transfers between devices: 25.7 us -> 20.1 us  [on_device(): dy_all = lax.all_gather(out_grad, 'node')]
    dot_general x3, matrix products: 23.6 us -> 18.6 us  [partial(): value = jnp.einsum(spec, rows, weight, preferred_element_type=jnp.float32)]
    all_gather x1, waiting for transfers between devices: 30.6 us -> 26.4 us  [on_device(): tok_all = lax.all_gather(tokens, 'node')]
  transfers between devices with their start and end apart: 3 -> 3, of which waited for: 3 -> 3; matrix products, arithmetic and copies ran while one was open for 10% -> 13% of each run, Pallas kernels for 0% -> 0%
where the time goes in v2:
time: 358 us
  Pallas kernels  200 us (56%)
  waiting for transfers between devices  69 us (19%)
  matrix products  57.8 us (16%)
  between operations  14 us (4%)
  blocking collectives  10.5 us (3%)
  local copies, waits for them, and re-layouts  3.8 us (1%)
    pallas_call x1, Pallas kernels, width_sum(): pl.pallas_call(functools.partial(width_sum_kernel, n, chunks, ch, 2, bloc...  200 us
    all_gather x1, waiting for transfers between devices, on_device(): tok_all = lax.all_gather(tokens, 'node')  26.4 us
    reduce_scatter x1, waiting for transfers between devices, on_device(): lax.psum_scatter(back, 'node', scatter_dimension=0, tiled=False)  21.8 us
    all_gather x1, waiting for transfers between devices, on_device(): dy_all = lax.all_gather(out_grad, 'node')  20.1 us
    dot_general x3, matrix products, partial(): value = jnp.einsum(spec, rows, weight, preferred_element_type=jnp.float32)  18.6 us
    all_gather x1, blocking collectives, on_device(): routing = lax.all_gather(routing, 'node')  10.5 us
    dot_general x1, matrix products, on_device(): jnp.einsum('erf,erd->efd', hidden_act, dy_flat, preferred_element_type=jn...  10.5 us
    dot_general x1, matrix products, on_device(): jnp.einsum('erd,erf->edf', x_flat, grad_gate, preferred_element_type=jnp....  8.05 us
  transfers between devices with their start and end apart: 3, of which 3 were waited for; matrix products, arithmetic and copies ran while one was open for 13% of the time, Pallas kernels for 0%

profile of v2, /device:TPU:0, one launch (start us, length us, event | category | flops | bytes accessed | tf_op | source)
XLA Modules:
  0.0 357.5 jit_solution(15273216502910253546)
XLA Ops:
  7.2 0.0 all-gather.6.cloned.1.call-start
  7.2 0.7 all-gather.6.cloned.1.call-update
  7.9 0.0 all-gather.8.cloned.1.call-start
  7.9 0.7 convert_element_type.42
  8.6 0.7 pad_maximum_fusion
  9.3 10.5 %all-gather = f32[1024,16]{0,1:T(8,128)S(1)} all-gather(f32[128,16]{0,1:T(8,128)S(1)} %pad_maximum_fusion), channel_id=2, replica_groups=mesh['node'=8,'local'=4] {'node'}, dimensions={0}, use_global_device_ids=true | all-gather | bytes 73728 | tf_op jit(solution)/shard_map/all_gather | solution.py:232
  19.9 0.0 all-gather.8.cloned.1.call-update
  19.9 0.0 reduce-scatter.2.cloned.1.call-start
  20.0 0.0 slice-start.2
  20.0 0.1 fusion.10
  20.1 0.1 compare_reduce_fusion
  20.2 0.1 fusion.6
  20.4 0.4 select_reduce_fusion
  20.8 26.4 %all-gather.6.cloned.1.call-done = bf16[1024,1792]{1,0:T(8,128)(2,1)} async-done(((bf16[128,1792]{1,0:T(8,128)(2,1)}), bf16[1024,1792]{1,0:T(8,128)(2,1)}) %all-gather.6.cloned.1.call-update) | async-done | bytes 3670032 | tf_op jit(solution)/shard_map/all_gather | solution.py:233
  47.1 3.5 convert_bitcast_fusion
  50.7 0.0 slice-start
  50.7 0.3 copy.29
  51.0 6.2 %convolution_convert_fusion.4 = bf16[2,640,1024]{2,1,0:T(8,128)(2,1)} fusion(bf16[2,640,1792]{2,1,0:T(8,128)(2,1)S(1)} %bitcast.56, bf16[2,1792,1024]{2,1,0:T(8,128)(2,1)S(1)} %bitcast.55), kind=kOutput, calls=%fused_computation.11 | convolution fusion | flops 4698931200 | bytes 14548992 | tf_op jit(solution)/shard_map/erd,edf->erf/dot_general | solution.py:256
  57.3 6.2 %convolution_convert_fusion.5 = bf16[2,640,1024]{2,1,0:T(8,128)(2,1)} fusion(bf16[2,640,1792]{2,1,0:T(8,128)(2,1)S(1)} %bitcast.57, bf16[2,1792,1024]{2,1,0:T(8,128)(2,1)S(1)} %bitcast.53), kind=kOutput, calls=%fused_computation.12 | convolution fusion | flops 4698931200 | bytes 14548992 | tf_op jit(solution)/shard_map/erd,edf->erf/dot_general | solution.py:256
  63.4 20.1 %all-gather.8.cloned.1.call-done = bf16[1024,1792]{1,0:T(8,128)(2,1)} async-done(((bf16[128,1792]{1,0:T(8,128)(2,1)}), bf16[1024,1792]{1,0:T(8,128)(2,1)}) %all-gather.8.cloned.1.call-update) | async-done | bytes 3670032 | tf_op jit(solution)/shard_map/all_gather | solution.py:235
  83.6 3.5 fusion
  87.1 0.0 slice-start.7
  87.1 0.3 copy.32
  87.4 3.1 slice-done.7
  90.5 6.2 %convolution_convert_fusion.3 = bf16[2,640,1024]{2,1,0:T(8,128)(2,1)} fusion(bf16[2,640,1792]{2,1,0:T(8,128)(2,1)S(1)} %bitcast.62, bf16[2,1024,1792]{2,1,0:T(8,128)(2,1)S(1)} %bitcast.72), kind=kOutput, calls=%fused_computation.10 | convolution fusion | flops 4698931200 | bytes 14548992 | tf_op jit(solution)/shard_map/erd,efd->erf/dot_general | solution.py:256
  96.8 200.4 %shard_map.102 = (bf16[1280,1024]{1,0:T(8,128)(2,1)}, bf16[1280,1024]{1,0:T(8,128)(2,1)}, bf16[1280,1024]{1,0:T(8,128)(2,1)}, bf16[1280,1792]{1,0:T(8,128)(2,1)}) custom-call(bf16[1280,1024]{1,0:T(8,128)(2,1)} %bitcast.67, bf16[1280,1024]{1,0:T(8,128)(2,1)} %bitcast.66, bf16[1280,1024]{1,0:T(8,128)(2,1)} %bitcast.68, bf16[2,1792,1024]{2,1,0:T(8,128)(2,1)} %gw_ref.1, ...), custom_call_target="tpu_custom_call" | custom-call | tf_op jit(solution)/shard_map/pallas_call | solution.py:196
  297.1 5.4 %bitcast_convert_fusion = bf16[8,128,1792]{2,1,0:T(8,128)(2,1)} fusion(bf16[2,8,80,1792]{3,2,1,0:T(8,128)(2,1)} %bitcast.64, s32[2,8,128]{2,0,1:T(2,128)S(1)} %copy.28), kind=kOutput, calls=%fused_computation.2 | convolution fusion | flops 589201408 | bytes 8265728 | tf_op jit(solution)/shard_map/ebst,ebsd->btd/dot_general | solution.py:280
  302.6 0.0 reduce-scatter.2.cloned.1.call-update
  302.6 10.5 %convolution_convert_fusion = bf16[2,1024,1792]{2,1,0:T(8,128)(2,1)} fusion(bf16[2,640,1024]{2,1,0:T(8,128)(2,1)S(1)} %bitcast.75, bf16[2,640,1792]{2,1,0:T(8,128)(2,1)} %bitcast.63), kind=kOutput, calls=%fused_computation.3 | convolution fusion | flops 4701290496 | bytes 14548992 | tf_op jit(solution)/shard_map/erf,erd->efd/dot_general | solution.py:288
  313.1 8.0 %convolution_convert_fusion.2 = bf16[2,1792,1024]{2,1,0:T(8,128)(2,1)} fusion(bf16[2,640,1792]{2,1,0:T(8,128)(2,1)S(1)} %bitcast.60, bf16[2,640,1024]{2,1,0:T(8,128)(2,1)S(1)} %bitcast.74), kind=kOutput, calls=%fused_computation.5 | convolution fusion | flops 4701290496 | bytes 14548992 | tf_op jit(solution)/shard_map/erd,erf->edf/dot_general | solution.py:291
  321.2 8.0 %convolution_convert_fusion.1 = bf16[2,1792,1024]{2,1,0:T(8,128)(2,1)} fusion(bf16[2,640,1792]{2,1,0:T(8,128)(2,1)S(1)} %bitcast.61, bf16[2,640,1024]{2,1,0:T(8,128)(2,1)S(1)} %bitcast.73), kind=kOutput, calls=%fused_computation.4 | convolution fusion | flops 4701290496 | bytes 14548992 | tf_op jit(solution)/shard_map/erd,erf->edf/dot_general | solution.py:294
  329.2 21.8 %reduce-scatter.2.cloned.1.call-done = bf16[1,128,1792]{2,1,0:T(8,128)(2,1)} async-done(((bf16[8,128,1792]{2,1,0:T(8,128)(2,1)}), bf16[1,128,1792]{2,1,0:T(8,128)(2,1)}) %reduce-scatter.2.cloned.1.call-update) | async-done | bytes 458768 | tf_op jit(solution)/shard_map/reduce_scatter | solution.py:286
  (33 shorter events, 0.1 us)
Async XLA Ops:
  7.2 40.0 %all-gather.6.cloned.1.call-start = ((), (), s32[]{:S(2)}) async-start(), calls=%async_computation.2 | async-start | bytes 4128768 | tf_op jit(solution)/shard_map/all_gather | solution.py:233
  7.9 75.7 %all-gather.8.cloned.1.call-start = ((), (), s32[]{:S(2)}) async-start(), calls=%async_computation.3 | async-start | bytes 4128768 | tf_op jit(solution)/shard_map/all_gather | solution.py:235
  19.9 331.1 %reduce-scatter.2.cloned.1.call-start = ((), (), s32[]{:S(2)}) async-start(), calls=%async_computation.1 | async-start | bytes 4128768 | tf_op jit(solution)/shard_map/reduce_scatter | solution.py:286
  20.0 31.0 %slice-start.2 = ((s8[7340032]{0:T(1024)(128)(4,1)}), s8[3145728]{0:T(1024)(128)(4,1)S(1)}, s32[]{:S(2)}) async-start(s8[7340032]{0:T(1024)(128)(4,1)} %bitcast.54), calls=%async_computation.6 | async-start | bytes 6291456
  47.1 3.9 %slice-start.3 = ((s8[7340032]{0:T(1024)(128)(4,1)}), s8[4194304]{0:T(1024)(128)(4,1)S(1)}, s32[]{:S(2)}) async-start(s8[7340032]{0:T(1024)(128)(4,1)} %bitcast.54), calls=%async_computation.7 | async-start | bytes 8388608
  50.7 6.6 %slice-start = ((s8[7340032]{0:T(1024)(128)(4,1)}), s8[3145728]{0:T(1024)(128)(4,1)S(1)}, s32[]{:S(2)}) async-start(s8[7340032]{0:T(1024)(128)(4,1)} %bitcast.52), calls=%async_computation.4 | async-start | bytes 6291456
  51.0 6.3 %copy-start = (bf16[2,8,80,1792]{3,2,1,0:T(8,128)(2,1)}, bf16[2,8,80,1792]{3,2,1,0:T(8,128)(2,1)S(1)}, u32[]{:S(2)}) copy-start(bf16[2,8,80,1792]{3,2,1,0:T(8,128)(2,1)S(1)} %copy.29) | copy-start | bytes 13762564
  51.0 6.2 %slice-start.1 = ((s8[7340032]{0:T(1024)(128)(4,1)}), s8[4194304]{0:T(1024)(128)(4,1)S(1)}, s32[]{:S(2)}) async-start(s8[7340032]{0:T(1024)(128)(4,1)} %bitcast.52), calls=%async_computation.5 | async-start | bytes 8388608
  83.6 3.9 %slice-start.6 = ((s8[7340032]{0:T(1024)(128)(4,1)}), s8[4194304]{0:T(1024)(128)(4,1)S(1)}, s32[]{:S(2)}) async-start(s8[7340032]{0:T(1024)(128)(4,1)} %bitcast.71), calls=%async_computation.10 | async-start | bytes 8388608
  87.1 3.4 slice-start.7
  87.4 9.3 %copy-start.1 = (bf16[2,8,80,1792]{3,2,1,0:T(8,128)(2,1)}, bf16[2,8,80,1792]{3,2,1,0:T(8,128)(2,1)S(1)}, u32[]{:S(2)}) copy-start(bf16[2,8,80,1792]{3,2,1,0:T(8,128)(2,1)S(1)} %copy.32) | copy-start | bytes 13762564
  297.1 5.5 %copy-start.4 = (bf16[1280,1024]{1,0:T(8,128)(2,1)S(1)}, bf16[1280,1024]{1,0:T(8,128)(2,1)}, u32[]{:S(2)}) copy-start(bf16[1280,1024]{1,0:T(8,128)(2,1)} %get-tuple-element.21) | copy-start | bytes 7864324
  302.6 10.6 %slice-start.4 = ((s8[4587520]{0:T(1024)(128)(4,1)}), s8[393216]{0:T(1024)(128)(4,1)S(1)}, s32[]{:S(2)}) async-start(s8[4587520]{0:T(1024)(128)(4,1)} %bitcast.58), calls=%async_computation.8 | async-start | bytes 786432
  302.6 10.5 %slice-start.5 = ((s8[4587520]{0:T(1024)(128)(4,1)}), s8[4194304]{0:T(1024)(128)(4,1)S(1)}, s32[]{:S(2)}) async-start(s8[4587520]{0:T(1024)(128)(4,1)} %bitcast.58), calls=%async_computation.9 | async-start | bytes 8388608
  302.6 10.5 %copy-start.3 = (bf16[1280,1024]{1,0:T(8,128)(2,1)S(1)}, bf16[1280,1024]{1,0:T(8,128)(2,1)}, u32[]{:S(2)}) copy-start(bf16[1280,1024]{1,0:T(8,128)(2,1)} %get-tuple-element.19) | copy-start | bytes 7864324
  313.1 8.1 %copy-start.2 = (bf16[1280,1024]{1,0:T(8,128)(2,1)S(1)}, bf16[1280,1024]{1,0:T(8,128)(2,1)}, u32[]{:S(2)}) copy-start(bf16[1280,1024]{1,0:T(8,128)(2,1)} %get-tuple-element.20) | copy-start | bytes 7864324
Sparse Core Ops, SparseCore 0:
  9.9 37.2 all-gather.5
  49.0 34.5 all-gather.7
  302.7 48.2 reduce-scatter.1

commit v3 on v2

--- a/solution.py
+++ b/solution.py
@@ -218,6 +218,78 @@
     )(gate_pre, up_pre, grad_hidden, gate_weight, up_weight)
 
 
+def gather_kernel(n, *refs):
+    count = 3
+    own, full = refs[:count], refs[count : 2 * count]
+    send, recv, pass_send, pass_recv, keep = refs[2 * count :]
+    me = lax.axis_index("node")
+    twin = me + 1 - 2 * lax.rem(me, 2)
+    peers = [lax.rem(me + 2 * d, n) for d in range(1, n // 2)]
+
+    barrier = pltpu.get_barrier_semaphore()
+    for peer in peers + [twin]:
+        pl.semaphore_signal(barrier, inc=1, device_id={"node": peer}, device_id_type=MESH)
+    pl.semaphore_wait(barrier, n // 2)
+
+    waits, arrivals, keeps = [], [], []
+    for i in range(count):
+        for d, peer in enumerate(peers):
+            copy = pltpu.make_async_remote_copy(
+                src_ref=own[i],
+                dst_ref=full[i].at[me],
+                send_sem=send.at[i, d],
+                recv_sem=recv.at[i, d],
+                device_id={"node": peer},
+                device_id_type=MESH,
+            )
+            copy.start()
+            arrivals.append((i, d, copy))
+        mine = pltpu.make_async_copy(own[i], full[i].at[me], keep.at[i])
+        mine.start()
+        keeps.append(mine)
+        copy = pltpu.make_async_remote_copy(
+            src_ref=own[i],
+            dst_ref=full[i].at[me],
+            send_sem=pass_send.at[i, 0],
+            recv_sem=pass_recv.at[i, 0],
+            device_id={"node": twin},
+            device_id_type=MESH,
+        )
+        copy.start()
+        waits.append(copy)
+    for i, d, copy in arrivals:
+        copy.wait_recv()
+        origin = lax.rem(me + n - 2 * (d + 1), n)
+        onward = pltpu.make_async_remote_copy(
+            src_ref=full[i].at[origin],
+            dst_ref=full[i].at[origin],
+            send_sem=pass_send.at[i, d + 1],
+            recv_sem=pass_recv.at[i, d + 1],
+            device_id={"node": twin},
+            device_id_type=MESH,
+        )
+        onward.start()
+        waits.append(onward)
+    for _, _, copy in arrivals:
+        copy.wait_send()
+    for copy in keeps + waits:
+        copy.wait()
+
+
+def gather_nodes(*own):
+    n = lax.axis_size("node")
+    anywhere = pl.BlockSpec(memory_space=pl.ANY)
+    sems = pltpu.SemaphoreType.DMA((len(own), n // 2))
+    return pl.pallas_call(
+        functools.partial(gather_kernel, n),
+        out_shape=tuple(jax.ShapeDtypeStruct((n,) + v.shape, v.dtype) for v in own),
+        in_specs=[anywhere] * len(own),
+        out_specs=(anywhere,) * len(own),
+        scratch_shapes=[sems] * 4 + [pltpu.SemaphoreType.DMA((len(own),))],
+        compiler_params=pltpu.CompilerParams(collective_id=1, has_side_effects=True),
+    )(*own)
+
+
 def on_device(tokens, out_grad, expert_ids, gates, gate_weight, up_weight, down_weight):
     tok_rows, slice_width = tokens.shape
     top_count = expert_ids.shape[1]
@@ -229,13 +301,11 @@
     row_count = node_count * capacity
 
     routing = jnp.concatenate([expert_ids.astype(jnp.float32), gates], axis=1)
-    routing = lax.all_gather(routing, "node")
-    tok_all = lax.all_gather(tokens, "node")
-    routing, out_grad = lax.optimization_barrier((routing, out_grad))
-    dy_all = lax.all_gather(out_grad, "node")
+    routing = jnp.pad(routing, ((0, 0), (0, 128 - 2 * top_count)))
+    routing, tok_all, dy_all = gather_nodes(routing, tokens, out_grad)
 
     ids_all = routing[:, :, :top_count].astype(jnp.int32)
-    gates_all = routing[:, :, top_count:]
+    gates_all = routing[:, :, top_count : 2 * top_count]
     mine = lax.axis_index("node") * exp_local + jnp.arange(exp_local, dtype=jnp.int32)
     hit = ids_all[None] == mine[:, None, None, None]
     named = jnp.any(hit, axis=3)
@@ -263,7 +333,6 @@
     )
     gate_pre = partial("erd,edf->erf", x_flat, gate_weight)
     up_pre = partial("erd,edf->erf", x_flat, up_weight)
-    gate_pre, up_pre, dy_all = lax.optimization_barrier((gate_pre, up_pre, dy_all))
     dy_flat = (
         (
             jnp.einsum("ebst,btd->ebsd", pick, dy_all, preferred_element_type=jnp.float32)

time: 358 us -> 355 us (level)
  Pallas kernels: 200 us -> 251 us
  waiting for transfers between devices: 69 us -> 22 us
  blocking collectives: 10.5 us -> 0 us
    pallas_call x0 -> x1, Pallas kernels: none -> 50.2 us  [gather_nodes(): pl.pallas_call(functools.partial(gather_kernel, n), out_shape=tuple((jax....]
    all_gather x2 -> x0, waiting for transfers between devices: 46.5 us -> none  [the longest x1 26.4 us: on_device(): tok_all = lax.all_gather(tokens, 'node')]
    all_gather x1 -> x0, blocking collectives: 10.5 us -> none  [on_device(): routing = lax.all_gather(routing, 'node')]
  transfers between devices with their start and end apart: 3 -> 1, of which waited for: 3 -> 1; matrix products, arithmetic and copies ran while one was open for 13% -> 7% of each run, Pallas kernels for 0% -> 0%
where the time goes in v3:
time: 355 us
  Pallas kernels  251 us (71%)
  matrix products  58.4 us (16%)
  waiting for transfers between devices  22 us (6%)
  between operations  14.2 us (4%)
  local copies, waits for them, and re-layouts  5.81 us (2%)
    pallas_call x1, Pallas kernels, width_sum(): pl.pallas_call(functools.partial(width_sum_kernel, n, chunks, ch, 2, bloc...  201 us
    pallas_call x1, Pallas kernels, gather_nodes(): pl.pallas_call(functools.partial(gather_kernel, n), out_shape=tuple((jax....  50.2 us
    reduce_scatter x1, waiting for transfers between devices, on_device(): lax.psum_scatter(back, 'node', scatter_dimension=0, tiled=False)  22 us
    dot_general x3, matrix products, partial(): value = jnp.einsum(spec, rows, weight, preferred_element_type=jnp.float32)  21.6 us
    dot_general x1, matrix products, on_device(): jnp.einsum('erf,erd->efd', hidden_act, dy_flat, preferred_element_type=jn...  10.5 us
    dot_general x1, matrix products, on_device(): jnp.einsum('erd,erf->edf', x_flat, grad_gate, preferred_element_type=jnp....  8.05 us
    dot_general x1, matrix products, on_device(): jnp.einsum('erd,erf->edf', x_flat, grad_up, preferred_element_type=jnp.fl...  8.02 us
  transfers between devices with their start and end apart: 1, of which 1 were waited for; matrix products, arithmetic and copies ran while one was open for 7% of the time, Pallas kernels for 0%

profile of v3, /device:TPU:0, one launch (start us, length us, event | category | flops | bytes accessed | tf_op | source)
XLA Modules:
  0.0 354.6 jit_solution(502453113212291573)
XLA Ops:
  7.2 0.0 reduce-scatter.2.cloned.1.call-start
  7.2 0.7 convert_element_type.44
  7.9 0.7 pad_maximum_fusion
  8.6 0.1 copy.46
  8.7 0.6 pad.4.refs_0_
  9.3 50.2 %shard_map.102 = (f32[8,128,128]{2,1,0:T(8,128)}, bf16[8,128,1792]{2,1,0:T(8,128)(2,1)}, bf16[8,128,1792]{2,1,0:T(8,128)(2,1)}) custom-call(f32[128,128]{1,0:T(8,128)} %pad.4.refs_0_, bf16[128,1792]{1,0:T(8,128)(2,1)} %refs_1_.1, bf16[128,1792]{1,0:T(8,128)(2,1)} %refs_2_.1), custom_call_target="tpu_custom_call" | custom-call | tf_op jit(solution)/shard_map/pallas_call | solution.py:283
  59.6 1.4 fusion.14
  61.0 0.2 copy.50
  61.2 0.2 copy.47
  61.3 0.1 compare_reduce_fusion
  61.5 0.1 fusion.11
  61.6 0.1 fusion.7
  61.7 0.4 select_reduce_fusion
  62.1 3.4 fusion
  65.5 0.0 slice-start.2
  65.5 2.6 copy.52
  68.1 1.0 copy-done.1
  69.2 1.3 convert_bitcast_fusion
  70.5 0.0 slice-start
  70.5 0.3 copy.49
  70.8 0.7 slice-done.3
  71.5 6.1 %convolution_convert_fusion.4 = bf16[2,640,1024]{2,1,0:T(8,128)(2,1)} fusion(bf16[2,640,1792]{2,1,0:T(8,128)(2,1)S(1)} %bitcast.49, bf16[2,1792,1024]{2,1,0:T(8,128)(2,1)S(1)} %bitcast.48), kind=kOutput, calls=%fused_computation.12 | convolution fusion | flops 4698931200 | bytes 14548992 | tf_op jit(solution)/shard_map/erd,edf->erf/dot_general | solution.py:326
  77.7 0.0 slice-start.7
  77.7 6.2 %convolution_convert_fusion.5 = bf16[2,640,1024]{2,1,0:T(8,128)(2,1)} fusion(bf16[2,640,1792]{2,1,0:T(8,128)(2,1)S(1)} %bitcast.50, bf16[2,1792,1024]{2,1,0:T(8,128)(2,1)S(1)} %bitcast.46), kind=kOutput, calls=%fused_computation.13 | convolution fusion | flops 4698931200 | bytes 14548992 | tf_op jit(solution)/shard_map/erd,edf->erf/dot_general | solution.py:326
  83.9 9.3 %convolution_convert_fusion.3 = bf16[2,640,1024]{2,1,0:T(8,128)(2,1)} fusion(bf16[2,640,1792]{2,1,0:T(8,128)(2,1)S(1)} %bitcast.58, bf16[2,1024,1792]{2,1,0:T(8,128)(2,1)} %param.13), kind=kOutput, calls=%fused_computation.11 | convolution fusion | flops 4698931200 | bytes 14548992 | tf_op jit(solution)/shard_map/erd,efd->erf/dot_general | solution.py:326
  93.2 200.5 %shard_map.103 = (bf16[1280,1024]{1,0:T(8,128)(2,1)}, bf16[1280,1024]{1,0:T(8,128)(2,1)}, bf16[1280,1024]{1,0:T(8,128)(2,1)}, bf16[1280,1792]{1,0:T(8,128)(2,1)}) custom-call(bf16[1280,1024]{1,0:T(8,128)(2,1)} %bitcast.61, bf16[1280,1024]{1,0:T(8,128)(2,1)} %bitcast.60, bf16[1280,1024]{1,0:T(8,128)(2,1)} %bitcast.62, bf16[2,1792,1024]{2,1,0:T(8,128)(2,1)} %gw_ref.1, ...), custom_call_target="tpu_custom_call" | custom-call | tf_op jit(solution)/shard_map/pallas_call | solution.py:196
  293.7 5.4 %bitcast_convert_fusion = bf16[8,128,1792]{2,1,0:T(8,128)(2,1)} fusion(bf16[2,8,80,1792]{3,2,1,0:T(8,128)(2,1)} %bitcast.59, s32[2,8,128]{2,0,1:T(2,128)S(1)} %copy.48), kind=kOutput, calls=%fused_computation.2 | convolution fusion | flops 589201408 | bytes 8265728 | tf_op jit(solution)/shard_map/ebst,ebsd->btd/dot_general | solution.py:349
  299.1 0.0 reduce-scatter.2.cloned.1.call-update
  299.2 10.5 %convolution_convert_fusion = bf16[2,1024,1792]{2,1,0:T(8,128)(2,1)} fusion(bf16[2,640,1024]{2,1,0:T(8,128)(2,1)S(1)} %bitcast.65, bf16[2,640,1792]{2,1,0:T(8,128)(2,1)} %bitcast.55), kind=kOutput, calls=%fused_computation.3 | convolution fusion | flops 4701290496 | bytes 14548992 | tf_op jit(solution)/shard_map/erf,erd->efd/dot_general | solution.py:357
  309.7 8.0 %convolution_convert_fusion.2 = bf16[2,1792,1024]{2,1,0:T(8,128)(2,1)} fusion(bf16[2,640,1792]{2,1,0:T(8,128)(2,1)S(1)} %bitcast.53, bf16[2,640,1024]{2,1,0:T(8,128)(2,1)S(1)} %bitcast.64), kind=kOutput, calls=%fused_computation.5 | convolution fusion | flops 4701290496 | bytes 14548992 | tf_op jit(solution)/shard_map/erd,erf->edf/dot_general | solution.py:360
  317.7 8.0 %convolution_convert_fusion.1 = bf16[2,1792,1024]{2,1,0:T(8,128)(2,1)} fusion(bf16[2,640,1792]{2,1,0:T(8,128)(2,1)S(1)} %bitcast.54, bf16[2,640,1024]{2,1,0:T(8,128)(2,1)S(1)} %bitcast.63), kind=kOutput, calls=%fused_computation.4 | convolution fusion | flops 4701290496 | bytes 14548992 | tf_op jit(solution)/shard_map/erd,erf->edf/dot_general | solution.py:363
  325.8 22.0 %reduce-scatter.2.cloned.1.call-done = bf16[1,128,1792]{2,1,0:T(8,128)(2,1)} async-done(((bf16[8,128,1792]{2,1,0:T(8,128)(2,1)}), bf16[1,128,1792]{2,1,0:T(8,128)(2,1)}) %reduce-scatter.2.cloned.1.call-update) | async-done | bytes 458768 | tf_op jit(solution)/shard_map/reduce_scatter | solution.py:355
  (28 shorter events, 0.1 us)
Async XLA Ops:
  7.2 340.6 %reduce-scatter.2.cloned.1.call-start = ((), (), s32[]{:S(2)}) async-start(), calls=%async_computation.1 | async-start | bytes 4128768 | tf_op jit(solution)/shard_map/reduce_scatter | solution.py:355
  65.5 3.7 %copy-start.1 = (bf16[8,128,1792]{2,1,0:T(8,128)(2,1)S(1)}, bf16[8,128,1792]{2,1,0:T(8,128)(2,1)}, u32[]{:S(2)}) copy-start(bf16[8,128,1792]{2,1,0:T(8,128)(2,1)} %get-tuple-element.12) | copy-start | bytes 11010052
  65.5 5.4 %slice-start.2 = ((s8[7340032]{0:T(1024)(128)(4,1)}), s8[4194304]{0:T(1024)(128)(4,1)S(1)}, s32[]{:S(2)}) async-start(s8[7340032]{0:T(1024)(128)(4,1)} %bitcast.47), calls=%async_computation.4 | async-start | bytes 8388608
  69.2 2.4 slice-start.3
  70.5 7.2 %slice-start = ((s8[7340032]{0:T(1024)(128)(4,1)}), s8[3145728]{0:T(1024)(128)(4,1)S(1)}, s32[]{:S(2)}) async-start(s8[7340032]{0:T(1024)(128)(4,1)} %bitcast.45), calls=%async_computation.2 | async-start | bytes 6291456
  70.8 6.9 %copy-start = (bf16[2,8,80,1792]{3,2,1,0:T(8,128)(2,1)}, bf16[2,8,80,1792]{3,2,1,0:T(8,128)(2,1)S(1)}, u32[]{:S(2)}) copy-start(bf16[2,8,80,1792]{3,2,1,0:T(8,128)(2,1)S(1)} %copy.49) | copy-start | bytes 13762564
  71.5 6.2 %slice-start.1 = ((s8[7340032]{0:T(1024)(128)(4,1)}), s8[4194304]{0:T(1024)(128)(4,1)S(1)}, s32[]{:S(2)}) async-start(s8[7340032]{0:T(1024)(128)(4,1)} %bitcast.45), calls=%async_computation.3 | async-start | bytes 8388608
  71.5 12.3 %slice-start.6 = ((s8[4587520]{0:T(1024)(128)(4,1)}), s8[4194304]{0:T(1024)(128)(4,1)S(1)}, s32[]{:S(2)}) async-start(s8[4587520]{0:T(1024)(128)(4,1)} %bitcast.56), calls=%async_computation.8 | async-start | bytes 8388608
  77.7 6.2 %slice-start.7 = ((s8[4587520]{0:T(1024)(128)(4,1)}), s8[393216]{0:T(1024)(128)(4,1)S(1)}, s32[]{:S(2)}) async-start(s8[4587520]{0:T(1024)(128)(4,1)} %bitcast.56), calls=%async_computation.9 | async-start | bytes 786432
  293.7 5.4 %copy-start.4 = (bf16[1280,1024]{1,0:T(8,128)(2,1)S(1)}, bf16[1280,1024]{1,0:T(8,128)(2,1)}, u32[]{:S(2)}) copy-start(bf16[1280,1024]{1,0:T(8,128)(2,1)} %get-tuple-element.17) | copy-start | bytes 7864324
  299.1 10.6 %slice-start.4 = ((s8[4587520]{0:T(1024)(128)(4,1)}), s8[393216]{0:T(1024)(128)(4,1)S(1)}, s32[]{:S(2)}) async-start(s8[4587520]{0:T(1024)(128)(4,1)} %bitcast.51), calls=%async_computation.6 | async-start | bytes 786432
  299.1 10.5 %slice-start.5 = ((s8[4587520]{0:T(1024)(128)(4,1)}), s8[4194304]{0:T(1024)(128)(4,1)S(1)}, s32[]{:S(2)}) async-start(s8[4587520]{0:T(1024)(128)(4,1)} %bitcast.51), calls=%async_computation.7 | async-start | bytes 8388608
  299.1 10.5 %copy-start.3 = (bf16[1280,1024]{1,0:T(8,128)(2,1)S(1)}, bf16[1280,1024]{1,0:T(8,128)(2,1)}, u32[]{:S(2)}) copy-start(bf16[1280,1024]{1,0:T(8,128)(2,1)} %get-tuple-element.15) | copy-start | bytes 7864324
  309.7 8.1 %copy-start.2 = (bf16[1280,1024]{1,0:T(8,128)(2,1)S(1)}, bf16[1280,1024]{1,0:T(8,128)(2,1)}, u32[]{:S(2)}) copy-start(bf16[1280,1024]{1,0:T(8,128)(2,1)} %get-tuple-element.16) | copy-start | bytes 7864324
Sparse Core Ops, SparseCore 0:
  299.2 48.4 reduce-scatter.1
